TPU v7x, 32 devices: a whole 2x2x4 slice. The times are simulated.
32 devices in a mesh: tm: 4 (over y, x), height: 2 (over core), head: 4 (over z).
Axes of the slice: x: 2, y: 2, z: 4, core: 2. Of those that a mesh axis runs over, the one named last changes fastest.
Arguments:
- queries: bfloat16 [4, 2, 128, 3072], P('tm', 'height', None, 'head'), may hold values from -8 to 8
- keys: bfloat16 [4, 2, 128, 3072], P('tm', 'height', None, 'head'), may hold values from -8 to 8
- values: bfloat16 [4, 2, 128, 3072], P('tm', 'height', None, 'head'), may hold values from -6 to 6
- grad_out: bfloat16 [4, 2, 128, 3072], P('tm', 'height', None, 'head'), may hold values from -6 to 6
- caption_keys: bfloat16 [256, 3072], P(None, 'head'), may hold values from -6 to 6
- caption_values: bfloat16 [256, 3072], P(None, 'head'), may hold values from -6 to 6
- caption_mask: int32 [256], replicated, may hold values 0 or 1
- kept: int32 [4, 2, 4], P('tm', 'height'), may hold values 0 or 1
Outputs:
- attended: bfloat16 [4, 2, 128, 3072], P('tm', 'height', None, 'head')
- query_grad: bfloat16 [4, 2, 128, 3072], P('tm', 'height', None, 'head')
- key_grad: bfloat16 [4, 2, 128, 3072], P('tm', 'height', None, 'head')
- value_grad: bfloat16 [4, 2, 128, 3072], P('tm', 'height', None, 'head')
- caption_key_grad: bfloat16 [256, 3072], P(None, 'head')
- caption_value_grad: bfloat16 [256, 3072], P(None, 'head')
All inputs are finite; a program needn't handle non-finite values. No bound on the sum of `kept` on one device may be relied on, other than what follows from the above.
Results may differ from a plain program's by a relative error of at most 0.029.
Values may be sent and summed in bfloat16 or wider, within the bound.
A program may use at most 64 MiB of HBM per device.

v0:
```python
import math

import jax
import jax.numpy as jnp
from jax import lax
from jax.sharding import PartitionSpec as P

HD = 128


def padded(block, sides, width):
    for axis, dim in sides:
        count = lax.axis_size(axis)
        forward = [(i, i + 1) for i in range(count - 1)]
        backward = [(target, source) for source, target in forward]
        low = lax.ppermute(
            lax.slice_in_dim(block, block.shape[dim] - width, None, axis=dim), axis, forward
        )
        high = lax.ppermute(lax.slice_in_dim(block, 0, width, axis=dim), axis, backward)
        block = jnp.concatenate([low, block, high], axis=dim)
    return block


def from_behind(shard, axis, by):
    count = lax.axis_size(axis)
    pairs = [(i, i + by) for i in range(count) if 0 <= i + by < count]
    return lax.ppermute(shard, axis, pairs)


def head_slice(array, start_head, head_group):
    picked = lax.slice_in_dim(
        array, start_head * HD, (start_head + head_group) * HD, axis=array.ndim - 1
    )
    return picked.reshape(picked.shape[:-1] + (head_group, HD))


def merge_heads(array):
    return array.reshape(array.shape[:-2] + (array.shape[-2] * array.shape[-1],))


def body(queries, keys, values, grad_out, caption_keys, caption_values, caption_mask, kept):
    score_scale = 1.0 / math.sqrt(HD)
    tile_rows = queries.shape[2]
    heads_here = queries.shape[3] // HD
    head_group = 2
    time_pos = lax.axis_index("tm")
    band_pos = lax.axis_index("height")
    inside = jnp.stack(
        [
            time_pos > 0,
            time_pos < lax.axis_size("tm") - 1,
            band_pos > 0,
            band_pos < lax.axis_size("height") - 1,
        ]
    )
    linked = (kept[0, 0] > 0) & inside
    packed = jnp.stack([keys, values])
    beside_all = padded(packed, (("tm", 1), ("height", 2)), 1)
    slots = ((0, 1), (2, 1), (1, 0), (1, 2))
    key_all = jnp.concatenate(
        [keys[0, 0]]
        + [beside_all[0, slot_time, slot_band] for slot_time, slot_band in slots]
        + [caption_keys],
        axis=0,
    )
    value_all = jnp.concatenate(
        [values[0, 0]]
        + [beside_all[1, slot_time, slot_band] for slot_time, slot_band in slots]
        + [caption_values],
        axis=0,
    )
    usable = jnp.concatenate(
        [jnp.ones((tile_rows,), jnp.bool_)]
        + [jnp.broadcast_to(linked[direction], (tile_rows,)) for direction in range(4)]
        + [caption_mask > 0]
    )
    own_queries = queries[0, 0]
    own_grads = grad_out[0, 0]
    out_parts, dquery_parts, dkey_parts, dvalue_parts, total_parts, delta_parts = (
        [],
        [],
        [],
        [],
        [],
        [],
    )
    for start_head in range(0, heads_here, head_group):
        query_heads = head_slice(own_queries, start_head, head_group)
        key_heads = head_slice(key_all, start_head, head_group)
        value_heads = head_slice(value_all, start_head, head_group)
        grad_heads = head_slice(own_grads, start_head, head_group)
        scores = (
            jnp.einsum("rgd,kgd->grk", query_heads, key_heads, preferred_element_type=jnp.float32)
            * score_scale
        )
        scores = jnp.where(usable, scores, -jnp.inf)
        row_top = jnp.max(scores, axis=-1, keepdims=True)
        log_total = row_top + jnp.log(jnp.sum(jnp.exp(scores - row_top), axis=-1, keepdims=True))
        weights = jnp.exp(scores - log_total)
        weights_half = weights.astype(jnp.bfloat16)
        out_heads = jnp.einsum(
            "grk,kgd->rgd", weights_half, value_heads, preferred_element_type=jnp.float32
        ).astype(jnp.bfloat16)
        row_delta = jnp.sum(
            out_heads.astype(jnp.float32) * grad_heads.astype(jnp.float32), axis=-1
        ).T[:, :, None]
        dweights = jnp.einsum(
            "rgd,kgd->grk", grad_heads, value_heads, preferred_element_type=jnp.float32
        )
        dscores = (weights * (dweights - row_delta)).astype(jnp.bfloat16)
        dquery = (
            jnp.einsum("grk,kgd->rgd", dscores, key_heads, preferred_element_type=jnp.float32)
            * score_scale
        )
        picked_scores, picked_weights = (dscores, weights_half)
        dkey = (
            jnp.einsum(
                "grk,rgd->kgd", picked_scores, query_heads, preferred_element_type=jnp.float32
            )
            * score_scale
        )
        dvalue = jnp.einsum(
            "grk,rgd->kgd", picked_weights, grad_heads, preferred_element_type=jnp.float32
        )
        out_parts.append(merge_heads(out_heads))
        dquery_parts.append(merge_heads(dquery.astype(jnp.bfloat16)))
        dkey_parts.append(merge_heads(dkey))
        dvalue_parts.append(merge_heads(dvalue))
        total_parts.append(log_total[:, :, 0])
        delta_parts.append(row_delta[:, :, 0])
    attended = jnp.concatenate(out_parts, axis=-1)
    query_grad = jnp.concatenate(dquery_parts, axis=-1)
    dkey_local = jnp.concatenate(dkey_parts, axis=-1)
    dvalue_local = jnp.concatenate(dvalue_parts, axis=-1)
    near = [
        jnp.stack(
            [
                dkey_local[(direction + 1) * tile_rows : (direction + 2) * tile_rows],
                dvalue_local[(direction + 1) * tile_rows : (direction + 2) * tile_rows],
            ]
        )
        for direction in range(4)
    ]
    from_later_time = from_behind(near[0].astype(jnp.bfloat16), "tm", -1).astype(jnp.float32)
    from_earlier_time = from_behind(near[1].astype(jnp.bfloat16), "tm", 1).astype(jnp.float32)
    from_upper_band = from_behind(near[2].astype(jnp.bfloat16), "height", -1).astype(jnp.float32)
    from_lower_band = from_behind(near[3].astype(jnp.bfloat16), "height", 1).astype(jnp.float32)
    arrived = from_later_time + from_earlier_time + from_upper_band + from_lower_band
    key_total = dkey_local[:tile_rows] + arrived[0]
    value_total = dvalue_local[:tile_rows] + arrived[1]
    caption_dk = dkey_local[5 * tile_rows :]
    caption_dv = dvalue_local[5 * tile_rows :]
    summed_keys, summed_values = lax.psum((caption_dk, caption_dv), ("tm", "height"))
    caption_key_grad = summed_keys.astype(jnp.bfloat16)
    caption_value_grad = summed_values.astype(jnp.bfloat16)
    tile_shape = queries.shape
    return (
        attended.reshape(tile_shape),
        query_grad.reshape(tile_shape),
        key_total.astype(jnp.bfloat16).reshape(tile_shape),
        value_total.astype(jnp.bfloat16).reshape(tile_shape),
        caption_key_grad,
        caption_value_grad,
    )


def solution(mesh):
    return jax.shard_map(
        body,
        mesh=mesh,
        in_specs=(
            P("tm", "height", None, "head"),
            P("tm", "height", None, "head"),
            P("tm", "height", None, "head"),
            P("tm", "height", None, "head"),
            P(None, "head"),
            P(None, "head"),
            P(),
            P("tm", "height", None),
        ),
        out_specs=(
            P("tm", "height", None, "head"),
            P("tm", "height", None, "head"),
            P("tm", "height", None, "head"),
            P("tm", "height", None, "head"),
            P(None, "head"),
            P(None, "head"),
        ),
        check_vma=False,
    )
```

profile of v0, /device:TPU:0, one launch (start us, length us, event | category | flops | bytes accessed | tf_op | source)
XLA Modules:
  0.0 161.3 jit_solution(11157962421260538889)
XLA Ops:
  0.7 1.1 copy.57
  3.0 4.9 %collective-permute-start = (bf16[2,1,1,128,768]{3,4,2,1,0:T(8,128)(2,1)S(1)}, bf16[2,1,1,128,768]{3,4,2,1,0:T(8,128)(2,1)S(1)}, u32[]{:S(2)}, u32[]{:S(2)}) collective-permute-start(bf16[2,1,1,128,768]{3,4,2,1,0:T(8,128)(2,1)S(1)} %pad_maximum_fusion.3), channel_id=1, source_target_pairs={{0,8},{8,16},{16,24},{1,9},{9,17},{17,25},{2,10},{10,18},{18,26},{... | collective-permute-start | bytes 1179656 | tf_op jit(solution)/shard_map/ppermute | solution.py:16
  7.8 1.3 collective-permute-start.1
  11.8 4.4 %collective-permute-done = bf16[2,1,1,128,768]{3,4,2,1,0:T(8,128)(2,1)S(1)} collective-permute-done((bf16[2,1,1,128,768]{3,4,2,1,0:T(8,128)(2,1)S(1)}, bf16[2,1,1,128,768]{3,4,2,1,0:T(8,128)(2,1)S(1)}, u32[]{:S(2)}, u32[]{:S(2)}) %collective-permute-start) | collective-permute-done | bytes 393248 | tf_op jit(solution)/shard_map/ppermute | solution.py:16
  16.2 10.4 %collective-permute-done.1 = bf16[2,1,1,128,768]{3,4,2,1,0:T(8,128)(2,1)S(1)} collective-permute-done((bf16[2,1,1,128,768]{3,4,2,1,0:T(8,128)(2,1)S(1)}, bf16[2,1,1,128,768]{3,4,2,1,0:T(8,128)(2,1)S(1)}, u32[]{:S(2)}, u32[]{:S(2)}) %collective-permute-start.1) | collective-permute-done | bytes 393248 | tf_op jit(solution)/shard_map/ppermute | solution.py:19
  26.5 1.2 pad_maximum_fusion.2
  27.7 2.3 %collective-permute-start.2 = (bf16[2,3,1,128,768]{3,4,2,1,0:T(8,128)(2,1)}, bf16[2,3,1,128,768]{3,4,2,1,0:T(8,128)(2,1)}, u32[]{:S(2)}, u32[]{:S(2)}) collective-permute-start(bf16[2,3,1,128,768]{3,4,2,1,0:T(8,128)(2,1)} %pad_maximum_fusion.2), channel_id=1, source_target_pairs={{0,4},{1,5},{2,6},{3,7},{8,12},{9,13},{10,14},{11,15},{16,20},{17,... | collective-permute-start | bytes 3538952 | tf_op jit(solution)/shard_map/ppermute | solution.py:16
  30.7 1.2 copy.64
  36.1 1.5 collective-permute-start.3
  43.7 1.6 %fusion.31 = bf16[896,768]{0,1:T(8,128)(2,1)} fusion(bf16[896,768]{0,1:T(8,128)(2,1)} %fusion.32, bf16[2,3,1,128,768]{3,4,2,1,0:T(8,128)(2,1)} %collective-permute-done.2), kind=kLoop, calls=%fused_computation.73 | loop fusion | bytes 393216
  45.3 1.6 %fusion.30 = bf16[896,768]{0,1:T(8,128)(2,1)} fusion(bf16[896,768]{0,1:T(8,128)(2,1)} %fusion.31, bf16[2,3,1,128,768]{3,4,2,1,0:T(8,128)(2,1)} %collective-permute-done.3), kind=kLoop, calls=%fused_computation.71 | loop fusion | bytes 393216
  47.8 1.4 fusion.45
  52.4 1.2 fusion
  56.3 1.2 fusion.1
  60.3 1.2 fusion.2
  61.5 2.5 %copy.103 = f32[896,2,128]{0,2,1:T(8,128)} copy(f32[896,2,128]{2,0,1:T(8,128)} %fusion) | data formatting | bytes 1835008 | tf_op jit(solution)/shard_map/mul | solution.py:117
  64.0 2.4 %copy.100 = f32[896,2,128]{0,2,1:T(8,128)} copy(f32[896,2,128]{2,0,1:T(8,128)} %fusion.1) | data formatting | bytes 1835008 | tf_op jit(solution)/shard_map/mul | solution.py:117
  66.4 2.4 %copy.97 = f32[896,2,128]{0,2,1:T(8,128)} copy(f32[896,2,128]{2,0,1:T(8,128)} %fusion.2) | data formatting | bytes 1835008 | tf_op jit(solution)/shard_map/mul | solution.py:117
  68.8 1.2 fusion.43
  71.0 1.3 fusion.44
  72.3 2.8 %pad_maximum_fusion = (f32[896,768]{0,1:T(8,128)}, f32[896,768]{0,1:T(8,128)}) fusion(f32[896,256]{0,1:T(8,128)S(1)} %bitcast.200, f32[896,256]{0,1:T(8,128)S(1)} %bitcast.202, f32[896,256]{0,1:T(8,128)S(1)} %bitcast.204, f32[896,256]{0,1:T(8,128)S(1)} %bitcast.194, f32[896,256]{0,1:T(8,128)S(1)} %bitcast.196, f32[896,256]{0,1:T(8,128)S(1)} %bitcast.198), kind=kLoop, calls=%fused_computation | loop fusion | flops 2752512 | bytes 11010048 | tf_op jit(solution)/shard_map/concatenate | solution.py:133
  79.5 1.6 slice_bitcast_fusion.8
  81.2 3.2 %collective-permute-start.7 = (bf16[2,128,768]{1,2,0:T(8,128)(2,1)S(1)}, bf16[2,128,768]{1,2,0:T(8,128)(2,1)S(1)}, u32[]{:S(2)}, u32[]{:S(2)}) collective-permute-start(bf16[2,128,768]{1,2,0:T(8,128)(2,1)S(1)} %pad_maximum_fusion.7), channel_id=1, source_target_pairs={{0,4},{1,5},{2,6},{3,7},{8,12},{9,13},{10,14},{11,15},{16,20},{17,... | collective-permute-start | bytes 1179656 | tf_op jit(solution)/shard_map/ppermute | solution.py:27
  85.2 1.3 collective-permute-start.6
  87.3 3.4 %collective-permute-start.5 = (bf16[2,128,768]{1,2,0:T(8,128)(2,1)}, bf16[2,128,768]{1,2,0:T(8,128)(2,1)S(1)}, u32[]{:S(2)}, u32[]{:S(2)}) collective-permute-start(bf16[2,128,768]{1,2,0:T(8,128)(2,1)} %pad_maximum_fusion.5), channel_id=1, source_target_pairs={{0,8},{8,16},{16,24},{1,9},{9,17},{17,25},{2,10},{10,18},{18,26},{... | collective-permute-start | bytes 1179656 | tf_op jit(solution)/shard_map/ppermute | solution.py:27
  91.5 1.3 collective-permute-start.4
  92.8 1.2 slice.192
  94.0 1.2 slice.193
  95.2 58.3 %all-reduce.2 = (bf16[256,768]{0,1:T(8,128)(2,1)}, bf16[256,768]{0,1:T(8,128)(2,1)}) all-reduce(f32[256,768]{0,1:T(8,128)S(1)} %slice.192, f32[256,768]{0,1:T(8,128)S(1)} %slice.193), channel_id=1, replica_groups=mesh['tm'=4,'height'=2,'head'=4] {'tm','height'}, use_global_device_ids=true, to_apply=%region_9.10 | all-reduce | flops 393216 | bytes 2359296 | tf_op jit(solution)/shard_map/psum | solution.py:153
  153.5 2.0 %copy.109 = bf16[256,768]{1,0:T(8,128)(2,1)} copy(bf16[256,768]{0,1:T(8,128)(2,1)} %get-tuple-element.12) | data formatting | bytes 786432
  155.5 1.9 %copy.110 = bf16[256,768]{1,0:T(8,128)(2,1)} copy(bf16[256,768]{0,1:T(8,128)(2,1)} %get-tuple-element.13) | data formatting | bytes 786432
  158.4 1.2 fusion.29
  (130 shorter events, 34.4 us)
Async XLA Ops:
  0.6 8.5 %copy-start.7 = (bf16[1,1,128,768]{3,2,1,0:T(8,128)(2,1)S(1)}, bf16[1,1,128,768]{3,2,1,0:T(8,128)(2,1)}, u32[]{:S(2)}) copy-start(bf16[1,1,128,768]{3,2,1,0:T(8,128)(2,1)} %param.10) | copy-start | bytes 589828
  0.6 8.5 %copy-start.19 = (bf16[1,1,128,768]{3,2,1,0:T(8,128)(2,1)S(1)}, bf16[1,1,128,768]{3,2,1,0:T(8,128)(2,1)}, u32[]{:S(2)}) copy-start(bf16[1,1,128,768]{3,2,1,0:T(8,128)(2,1)} %param.11) | copy-start | bytes 589828
  1.8 9.2 %copy-start.21 = (s32[256]{0:T(256)S(1)}, s32[256]{0:T(256)}, u32[]{:S(2)}) copy-start(s32[256]{0:T(256)} %param.14) | copy-start | bytes 3076
  1.8 9.2 %copy-start.20 = (s32[1,1,4]{2,1,0:T(1,128)S(1)}, s32[1,1,4]{2,1,0:T(1,128)}, u32[]{:S(2)}) copy-start(s32[1,1,4]{2,1,0:T(1,128)} %param.15) | copy-start | bytes 52
  3.0 13.2 %collective-permute-start = (bf16[2,1,1,128,768]{3,4,2,1,0:T(8,128)(2,1)S(1)}, bf16[2,1,1,128,768]{3,4,2,1,0:T(8,128)(2,1)S(1)}, u32[]{:S(2)}, u32[]{:S(2)}) collective-permute-start(bf16[2,1,1,128,768]{3,4,2,1,0:T(8,128)(2,1)S(1)} %pad_maximum_fusion.3), channel_id=1, source_target_pairs={{0,8},{8,16},{16,24},{1,9},{9,17},{17,25},{2,10},{10,18},{18,26},{... | collective-permute-start | bytes 1179656 | tf_op jit(solution)/shard_map/ppermute | solution.py:16
  7.8 18.7 %collective-permute-start.1 = (bf16[2,1,1,128,768]{3,4,2,1,0:T(8,128)(2,1)S(1)}, bf16[2,1,1,128,768]{3,4,2,1,0:T(8,128)(2,1)S(1)}, u32[]{:S(2)}, u32[]{:S(2)}) collective-permute-start(bf16[2,1,1,128,768]{3,4,2,1,0:T(8,128)(2,1)S(1)} %pad_maximum_fusion.3), channel_id=1, source_target_pairs={{8,0},{16,8},{24,16},{9,1},{17,9},{25,17},{10,2},{18,10},{26,18},{... | collective-permute-start | bytes 1179656 | tf_op jit(solution)/shard_map/ppermute | solution.py:19
  27.7 11.7 %collective-permute-start.2 = (bf16[2,3,1,128,768]{3,4,2,1,0:T(8,128)(2,1)}, bf16[2,3,1,128,768]{3,4,2,1,0:T(8,128)(2,1)}, u32[]{:S(2)}, u32[]{:S(2)}) collective-permute-start(bf16[2,3,1,128,768]{3,4,2,1,0:T(8,128)(2,1)} %pad_maximum_fusion.2), channel_id=1, source_target_pairs={{0,4},{1,5},{2,6},{3,7},{8,12},{9,13},{10,14},{11,15},{16,20},{17,... | collective-permute-start | bytes 3538952 | tf_op jit(solution)/shard_map/ppermute | solution.py:16
  36.1 5.1 %collective-permute-start.3 = (bf16[2,3,1,128,768]{3,4,2,1,0:T(8,128)(2,1)}, bf16[2,3,1,128,768]{3,4,2,1,0:T(8,128)(2,1)}, u32[]{:S(2)}, u32[]{:S(2)}) collective-permute-start(bf16[2,3,1,128,768]{3,4,2,1,0:T(8,128)(2,1)} %pad_maximum_fusion.2), channel_id=1, source_target_pairs={{4,0},{5,1},{6,2},{7,3},{12,8},{13,9},{14,10},{15,11},{20,16},{21,... | collective-permute-start | bytes 3538952 | tf_op jit(solution)/shard_map/ppermute | solution.py:19
  38.7 3.6 %copy-start.9 = (bf16[256,768]{1,0:T(8,128)(2,1)S(1)}, bf16[256,768]{1,0:T(8,128)(2,1)}, u32[]{:S(2)}) copy-start(bf16[256,768]{1,0:T(8,128)(2,1)} %param.13) | copy-start | bytes 1179652
  47.8 1.5 copy-start.8
  49.2 8.5 %copy-start.3 = (bf16[896,256]{0,1:T(8,128)(2,1)}, bf16[896,256]{0,1:T(8,128)(2,1)S(1)}, u32[]{:S(2)}) copy-start(bf16[896,256]{0,1:T(8,128)(2,1)S(1)} %get-tuple-element.22) | copy-start | bytes 1376260
  51.4 2.1 %copy-start.6 = (bf16[896,256]{1,0:T(8,128)(2,1)S(1)}, bf16[896,256]{1,0:T(8,128)(2,1)}, u32[]{:S(2)}) copy-start(bf16[896,256]{1,0:T(8,128)(2,1)} %get-tuple-element.27) | copy-start | bytes 1376260
  55.4 2.1 %copy-start.5 = (bf16[896,256]{1,0:T(8,128)(2,1)S(1)}, bf16[896,256]{1,0:T(8,128)(2,1)}, u32[]{:S(2)}) copy-start(bf16[896,256]{1,0:T(8,128)(2,1)} %get-tuple-element.25) | copy-start | bytes 1376260
  59.0 1.0 copy-start.4
  68.8 1.5 copy-start
  68.8 1.9 %copy-start.1 = (f32[896,2,128]{0,2,1:T(8,128)S(1)}, f32[896,2,128]{0,2,1:T(8,128)}, u32[]{:S(2)}) copy-start(f32[896,2,128]{0,2,1:T(8,128)} %copy.100) | copy-start | bytes 2752516
  68.8 2.2 %copy-start.2 = (f32[896,2,128]{0,2,1:T(8,128)S(1)}, f32[896,2,128]{0,2,1:T(8,128)}, u32[]{:S(2)}) copy-start(f32[896,2,128]{0,2,1:T(8,128)} %copy.97) | copy-start | bytes 2752516
  72.3 2.8 %copy-start.10 = (bf16[2,128,128]{2,1,0:T(8,128)(2,1)S(1)}, bf16[2,128,128]{2,1,0:T(8,128)(2,1)}, u32[]{:S(2)}) copy-start(bf16[2,128,128]{2,1,0:T(8,128)(2,1)} %get-tuple-element.47) | copy-start | bytes 196612
  72.3 5.0 %copy-start.17 = (bf16[2,128,128]{2,1,0:T(8,128)(2,1)S(1)}, bf16[2,128,128]{2,1,0:T(8,128)(2,1)}, u32[]{:S(2)}) copy-start(bf16[2,128,128]{2,1,0:T(8,128)(2,1)} %fusion.20) | copy-start | bytes 196612
  72.3 5.7 %copy-start.18 = (bf16[2,128,128]{2,1,0:T(8,128)(2,1)S(1)}, bf16[2,128,128]{2,1,0:T(8,128)(2,1)}, u32[]{:S(2)}) copy-start(bf16[2,128,128]{2,1,0:T(8,128)(2,1)} %fusion.19) | copy-start | bytes 196612
  81.2 77.0 %collective-permute-start.7 = (bf16[2,128,768]{1,2,0:T(8,128)(2,1)S(1)}, bf16[2,128,768]{1,2,0:T(8,128)(2,1)S(1)}, u32[]{:S(2)}, u32[]{:S(2)}) collective-permute-start(bf16[2,128,768]{1,2,0:T(8,128)(2,1)S(1)} %pad_maximum_fusion.7), channel_id=1, source_target_pairs={{0,4},{1,5},{2,6},{3,7},{8,12},{9,13},{10,14},{11,15},{16,20},{17,... | collective-permute-start | bytes 1179656 | tf_op jit(solution)/shard_map/ppermute | solution.py:27
  85.2 73.0 %collective-permute-start.6 = (bf16[2,128,768]{1,2,0:T(8,128)(2,1)}, bf16[2,128,768]{1,2,0:T(8,128)(2,1)S(1)}, u32[]{:S(2)}, u32[]{:S(2)}) collective-permute-start(bf16[2,128,768]{1,2,0:T(8,128)(2,1)} %pad_maximum_fusion.6), channel_id=1, source_target_pairs={{4,0},{5,1},{6,2},{7,3},{12,8},{13,9},{14,10},{15,11},{20,16},{21,... | collective-permute-start | bytes 1179656 | tf_op jit(solution)/shard_map/ppermute | solution.py:27
  87.3 70.9 %collective-permute-start.5 = (bf16[2,128,768]{1,2,0:T(8,128)(2,1)}, bf16[2,128,768]{1,2,0:T(8,128)(2,1)S(1)}, u32[]{:S(2)}, u32[]{:S(2)}) collective-permute-start(bf16[2,128,768]{1,2,0:T(8,128)(2,1)} %pad_maximum_fusion.5), channel_id=1, source_target_pairs={{0,8},{8,16},{16,24},{1,9},{9,17},{17,25},{2,10},{10,18},{18,26},{... | collective-permute-start | bytes 1179656 | tf_op jit(solution)/shard_map/ppermute | solution.py:27
  91.5 66.7 %collective-permute-start.4 = (bf16[2,128,768]{1,2,0:T(8,128)(2,1)}, bf16[2,128,768]{1,2,0:T(8,128)(2,1)S(1)}, u32[]{:S(2)}, u32[]{:S(2)}) collective-permute-start(bf16[2,128,768]{1,2,0:T(8,128)(2,1)} %pad_maximum_fusion.4), channel_id=1, source_target_pairs={{8,0},{16,8},{24,16},{9,1},{17,9},{25,17},{10,2},{18,10},{26,18},{... | collective-permute-start | bytes 1179656 | tf_op jit(solution)/shard_map/ppermute | solution.py:27
  153.5 3.9 %copy-start.11 = (bf16[128,256]{1,0:T(8,128)(2,1)S(1)}, bf16[128,256]{1,0:T(8,128)(2,1)}, u32[]{:S(2)}) copy-start(bf16[128,256]{1,0:T(8,128)(2,1)} %copy.79) | copy-start | bytes 196612
  153.5 3.9 %copy-start.12 = (bf16[128,256]{1,0:T(8,128)(2,1)S(1)}, bf16[128,256]{1,0:T(8,128)(2,1)}, u32[]{:S(2)}) copy-start(bf16[128,256]{1,0:T(8,128)(2,1)} %copy.78) | copy-start | bytes 196612
  153.5 3.9 %copy-start.13 = (bf16[128,256]{1,0:T(8,128)(2,1)S(1)}, bf16[128,256]{1,0:T(8,128)(2,1)}, u32[]{:S(2)}) copy-start(bf16[128,256]{1,0:T(8,128)(2,1)} %copy.77) | copy-start | bytes 196612
  153.5 3.9 %copy-start.14 = (bf16[128,256]{1,0:T(8,128)(2,1)S(1)}, bf16[128,256]{1,0:T(8,128)(2,1)}, u32[]{:S(2)}) copy-start(bf16[128,256]{1,0:T(8,128)(2,1)} %copy.94) | copy-start | bytes 196612
  153.5 3.9 %copy-start.15 = (bf16[128,256]{1,0:T(8,128)(2,1)S(1)}, bf16[128,256]{1,0:T(8,128)(2,1)}, u32[]{:S(2)}) copy-start(bf16[128,256]{1,0:T(8,128)(2,1)} %copy.93) | copy-start | bytes 196612
  153.5 3.9 %copy-start.16 = (bf16[128,256]{1,0:T(8,128)(2,1)S(1)}, bf16[128,256]{1,0:T(8,128)(2,1)}, u32[]{:S(2)}) copy-start(bf16[128,256]{1,0:T(8,128)(2,1)} %copy.92) | copy-start | bytes 196612
where the time goes:
time: 164 us; the launch traced here: 161 us
  blocking collectives  58.3 us (36%)
  local copies, waits for them, and re-layouts  45.1 us (28%)
  starting transfers between devices  19.1 us (12%)
  waiting for transfers between devices  15.5 us (9%)
  other arithmetic  11.6 us (7%)
  matrix products  10.5 us (6%)
    psum x1, blocking collectives, body(): lax.psum((caption_dk, caption_dv), ('tm', 'height'))  58.3 us
    unnamed x67, local copies, waits for them, and re-layouts  18.4 us
    ppermute x2, waiting for transfers between devices, padded(): lax.ppermute(lax.slice_in_dim(block, 0, width, axis=dim), axis, backward)  11 us
    ppermute x4, starting transfers between devices, from_behind(): return lax.ppermute(shard, axis, pairs)  9.19 us
    mul x3, local copies, waits for them, and re-layouts, body(): jnp.einsum('grk,rgd->kgd', picked_scores, query_heads, preferred_element_...  7.3 us
    ppermute x2, starting transfers between devices, padded(): lax.ppermute(lax.slice_in_dim(block, block.shape[dim] - width, None, axis...  7.16 us
    reshape x6, local copies, waits for them, and re-layouts, merge_heads(): array.reshape(array.shape[:-2] + (array.shape[-2] * array.shape[-1],))  4.45 us
    ppermute x2, waiting for transfers between devices, padded(): lax.ppermute(lax.slice_in_dim(block, block.shape[dim] - width, None, axis...  4.42 us
  transfers between devices with their start and end apart: 8, of which 3 were waited for; matrix products, arithmetic and copies ran while one was open for 13% of the time, Pallas kernels for 0%

commit v1 on v0

v1 whole, which is shorter than its diff:
```python
import functools
import math

import jax
import jax.numpy as jnp
from jax import lax
from jax.experimental import pallas as pl
from jax.experimental.pallas import tpu as pltpu
from jax.sharding import PartitionSpec as P

HD = 128
NEG = -1e30
F32 = jnp.float32
BF16 = jnp.bfloat16
MESH = pl.DeviceIdType.MESH


class Plan:
    def __init__(self, mesh_shape, tile, cap, heads):
        self.pairs = mesh_shape["tm"] // 2
        self.bands = mesh_shape["height"]
        self.tile, self.cap, self.heads = tile, cap, heads
        self.group = heads // 2
        self.sides = 1 if self.bands == 2 else 2
        self.lo_side = [tile * (1 + j) for j in range(self.sides)]
        self.lo = tile * (1 + self.sides)
        self.hi = self.lo + tile
        self.caps = self.hi + tile
        self.hi_side = [self.caps + cap + tile * j for j in range(self.sides)]
        self.next = self.caps + cap + tile * self.sides
        self.rows = self.next + tile
        self.span = self.caps + cap
        self.inside = self.pairs == 2 and self.bands == 2 and cap % 64 == 0
        self.part = cap // 4
        self.kinds = {}

    def opposite(self, j):
        return 0 if self.sides == 1 else 1 - j

    def number(self, kind, i):
        base = self.kinds.setdefault(kind, len(self.kinds))
        return base * self.group + i


def kernel(plan, scale, q_in, k_in, v_in, g_in, ck_in, cv_in, mask_ref, kept_ref,
           o_att, o_dq, o_dk, o_dv, o_ck, o_cv,
           kb, vb, qb, gb, links, acc, caps, cs, cr, cp, crv, fp, fs, ats,
           local_sem, send_sem, recv_sem):
    T, G, C = plan.tile, plan.group, plan.cap
    tm, band, head = lax.axis_index("tm"), lax.axis_index("height"), lax.axis_index("head")
    s, k = lax.rem(tm, 2), lax.div(tm, 2)
    up_ok, down_ok = k < plan.pairs - 1, k > 0
    partner = (tm + 1 - 2 * s, band, head)
    above, below = (tm + 2, band, head), (tm - 2, band, head)
    if plan.sides == 1:
        side_dev = [(tm, 1 - band, head)]
        side_ok = [None]
    else:
        side_dev = [(tm, band - 1, head), (tm, band + 1, head)]
        side_ok = [band > 0, band < plan.bands - 1]

    def when(ok, fn):
        if ok is None:
            fn()
        else:
            pl.when(ok)(fn)

    def both(a, b):
        return b if a is None else a & b

    def mine(i):
        return pl.ds(pl.multiple_of((s * G + i) * HD, HD), HD)

    def his(i):
        return pl.ds(pl.multiple_of(((1 - s) * G + i) * HD, HD), HD)

    def rows(start, size=T):
        return pl.ds(pl.multiple_of(start, 16), size)

    own_slot, his_slot = rows(plan.lo + s * T), rows(plan.lo + (1 - s) * T)

    def side_slot(j, t):
        return rows(plan.lo_side[j] + t * (plan.hi_side[j] - plan.lo_side[j]))

    def remote(kind, i, src, dst, dev):
        n = plan.number(kind, i)
        return pltpu.make_async_remote_copy(
            src_ref=src, dst_ref=dst, send_sem=send_sem.at[n], recv_sem=recv_sem.at[n],
            device_id=dev, device_id_type=MESH)

    sends = []

    def start(ok, copy):
        when(ok, copy.start)
        sends.append((ok, copy))

    own_kv, own_qg = [], []
    for i in range(G):
        group = [
            (k_in.at[0, 0, :, mine(i)], kb.at[i, own_slot]),
            (v_in.at[0, 0, :, mine(i)], vb.at[i, own_slot]),
            (q_in.at[0, 0, :, mine(i)], qb.at[i, rows(s * T)]),
            (g_in.at[0, 0, :, mine(i)], gb.at[i, rows(s * T)]),
            (ck_in.at[:, mine(i)], kb.at[i, pl.ds(plan.caps, C)]),
            (cv_in.at[:, mine(i)], vb.at[i, pl.ds(plan.caps, C)]),
        ]
        made = [pltpu.make_async_copy(a, b, local_sem.at[6 * i + n]) for n, (a, b) in enumerate(group)]
        for copy in made:
            copy.start()
        own_kv.append(made[:2])
        own_qg.append(made[2:])

    def clear(at, rows_at):
        for i in range(G):
            kb[i, pl.ds(at, T)] = jnp.zeros((T, HD), BF16)
            vb[i, pl.ds(at, T)] = jnp.zeros((T, HD), BF16)
            cr[i, pl.ds(rows_at, T)] = jnp.zeros((T, 2 * HD), BF16)

    pl.when(k == 0)(lambda: clear(0, T))
    pl.when(k == plan.pairs - 1)(lambda: clear(plan.next, 0))
    for j in range(plan.sides):
        if side_ok[j] is not None:
            def clear_side(j=j):
                clear(plan.lo_side[j], 2 * T + 2 * T * j)
                clear(plan.hi_side[j], 3 * T + 2 * T * j)
            pl.when(jnp.logical_not(side_ok[j]))(clear_side)

    time_ok = [tm > 0, tm < 2 * plan.pairs - 1]
    for row in range(2 + plan.sides):
        if row < 2:
            linked = (kept_ref[0, 0, row] > 0) & time_ok[row]
        elif plan.sides == 1:
            linked = kept_ref[0, 0, 3 - band] > 0
        else:
            linked = (kept_ref[0, 0, row] > 0) & side_ok[row - 2]
        links[s, pl.ds(row, 1), :] = jnp.broadcast_to(
            jnp.where(linked, 0.0, NEG).astype(F32), (1, 128))

    barrier = pltpu.get_barrier_semaphore()
    peers = [(None, partner), (up_ok, above), (down_ok, below)]
    peers += [(side_ok[j], side_dev[j]) for j in range(plan.sides)]
    if plan.inside:
        across = lax.rem(tm + 2, 4)
        mates = [(tm, 1 - band, head), (across, band, head), (across, 1 - band, head)]
        peers.append((None, mates[2]))
    for ok, dev in peers:
        when(ok, functools.partial(pl.semaphore_signal, barrier, inc=1, device_id=dev,
                                   device_id_type=MESH))
    pl.semaphore_wait(barrier, sum(1 if ok is None else ok.astype(jnp.int32) for ok, _ in peers))

    link_copy = remote("link", 0, links.at[s], links.at[s], partner)
    start(None, link_copy)
    swap_kv, swap_qg = [], []
    for i in range(G):
        made = [remote("k", i, k_in.at[0, 0, :, his(i)], kb.at[i, own_slot], partner),
                remote("v", i, v_in.at[0, 0, :, his(i)], vb.at[i, own_slot], partner)]
        for copy in made:
            start(None, copy)
        swap_kv.append(made)
    for i in range(G):
        made = [remote("q", i, q_in.at[0, 0, :, his(i)], qb.at[i, rows(s * T)], partner),
                remote("g", i, g_in.at[0, 0, :, his(i)], gb.at[i, rows(s * T)], partner)]
        for copy in made:
            start(None, copy)
        swap_qg.append(made)

    up, down = [], []
    side_first = [[] for _ in range(plan.sides)]
    side_second = [[] for _ in range(plan.sides)]
    for i in range(G):
        up.append([remote("up" + n, i, b.at[i, pl.ds(plan.hi, T)], b.at[i, pl.ds(0, T)], above)
                   for n, b in (("k", kb), ("v", vb))])
        down.append([remote("down" + n, i, b.at[i, pl.ds(plan.lo, T)], b.at[i, pl.ds(plan.next, T)], below)
                     for n, b in (("k", kb), ("v", vb))])
        for j in range(plan.sides):
            o = plan.opposite(j)
            side_first[j].append([
                remote("first%d%s" % (o, n), i, b.at[i, own_slot], b.at[i, side_slot(o, s)], side_dev[j])
                for n, b in (("k", kb), ("v", vb))])
            side_second[j].append([
                remote("second%d%s" % (o, n), i, b.at[i, his_slot], b.at[i, side_slot(o, 1 - s)], side_dev[j])
                for n, b in (("k", kb), ("v", vb))])

    def begin(ok, pair):
        def go():
            for copy in pair:
                copy.start()
        when(ok, go)

    for i in range(G):
        for copy in own_kv[i]:
            copy.wait()
        begin(up_ok & (s == 1), up[i])
        begin(down_ok & (s == 0), down[i])
        for j in range(plan.sides):
            begin(side_ok[j], side_first[j][i])
    for i in range(G):
        for copy in swap_kv[i]:
            copy.wait_recv()
        begin(up_ok & (s == 0), up[i])
        begin(down_ok & (s == 1), down[i])
        for j in range(plan.sides):
            begin(side_ok[j], side_second[j][i])
    for i in range(G):
        sends.extend((up_ok, c) for c in up[i])
        sends.extend((down_ok, c) for c in down[i])
        for j in range(plan.sides):
            sends.extend((side_ok[j], c) for c in side_first[j][i] + side_second[j][i])

    def arrived(ok, pair):
        def go():
            for copy in pair:
                copy.wait_recv()
        when(ok, go)

    link_copy.wait_recv()
    cap_off = jnp.where(mask_ref[...] > 0, 0.0, NEG).astype(F32)
    zero_off = jnp.zeros((1, T), F32)

    def row_of(t, r):
        return links[t, r:r + 1, :]

    side_rows = range(2, 2 + plan.sides)
    offsets = [
        jnp.concatenate([row_of(0, 0)] + [row_of(0, r) for r in side_rows]
                        + [zero_off, row_of(0, 1), cap_off], axis=1),
        jnp.concatenate([row_of(1, 0), zero_off, cap_off]
                        + [row_of(1, r) for r in side_rows] + [row_of(1, 1)], axis=1),
    ]

    def dot(a, b, dims):
        return lax.dot_general(a, b, (dims, ((), ())), preferred_element_type=F32)

    last_recv = []
    returns = {}

    def attend(i):
        for copy in own_qg[i]:
            copy.wait()
        for copy in swap_qg[i]:
            copy.wait_recv()
        arrived(down_ok, up[i])
        arrived(up_ok, down[i])
        for j in range(plan.sides):
            arrived(side_ok[j], side_first[plan.opposite(j)][i] + side_second[plan.opposite(j)][i])
        grads = []
        for t in range(2):
            span = pl.ds(0 if t == 0 else plan.lo, plan.span)
            keys, values = kb[i, span, :], vb[i, span, :]
            query, grad = qb[i, pl.ds(t * T, T), :], gb[i, pl.ds(t * T, T), :]
            scores = dot(query, keys, ((1,), (1,))) * scale + offsets[t]
            top = jnp.max(scores, axis=-1, keepdims=True)
            weights = jnp.exp(scores - top)
            weights = weights * (1.0 / jnp.sum(weights, axis=-1, keepdims=True))
            half = weights.astype(BF16)
            out = dot(half, values, ((1,), (0,))).astype(BF16)
            ats[i, 0, pl.ds(t * T, T), :] = out
            delta = jnp.sum(out.astype(F32) * grad.astype(F32), axis=-1, keepdims=True)
            dweights = dot(grad, values, ((1,), (1,)))
            dscores = (weights * (dweights - delta)).astype(BF16)
            ats[i, 1, pl.ds(t * T, T), :] = (dot(dscores, keys, ((1,), (0,))) * scale).astype(BF16)
            dk = dot(dscores, query, ((0,), (0,))) * scale
            dv = dot(half, grad, ((0,), (0,)))
            grads.append(jnp.concatenate([dk, dv], axis=1))
        made = [remote("att", i, ats.at[i, 0, rows((1 - s) * T)], o_att.at[0, 0, :, mine(i)], partner),
                remote("dq", i, ats.at[i, 1, rows((1 - s) * T)], o_dq.at[0, 0, :, mine(i)], partner)]
        for copy in made:
            start(None, copy)
            last_recv.append(copy)
        low, high = grads
        mid = plan.lo
        cs[i, pl.ds(0, T), :] = low[:T].astype(BF16)
        cs[i, pl.ds(T, T), :] = high[plan.span - T:].astype(BF16)
        for j in range(plan.sides):
            at = 2 * T + 2 * T * j
            cs[i, pl.ds(at, T), :] = low[plan.lo_side[j]:plan.lo_side[j] + T].astype(BF16)
            hs = plan.hi_side[j] - mid
            cs[i, pl.ds(at + T, T), :] = high[hs:hs + T].astype(BF16)
        to_below = remote("rb", i, cs.at[i, pl.ds(0, T)], cr.at[i, pl.ds(0, T)], below)
        to_above = remote("ra", i, cs.at[i, pl.ds(T, T)], cr.at[i, pl.ds(T, T)], above)
        start(down_ok, to_below)
        start(up_ok, to_above)
        to_side = []
        for j in range(plan.sides):
            o = plan.opposite(j)
            copy = remote("rs%d" % o, i, cs.at[i, pl.ds(2 * T + 2 * T * j, 2 * T)],
                          cr.at[i, pl.ds(2 * T + 2 * T * o, 2 * T)], side_dev[j])
            start(side_ok[j], copy)
            to_side.append(copy)
        shared = low[mid:] + high[:plan.span - mid]
        tail = shared[2 * T:]
        if plan.inside:
            caps[i] = tail
            cp[i] = tail.astype(BF16)
            numbers = [2 * k + 1 - band, 2 * (1 - k) + band, 2 * (1 - k) + 1 - band]
            rs = [remote("cr%d" % n, i, cp.at[i, rows(numbers[n] * plan.part, plan.part)],
                         crv.at[i, n], mates[n]) for n in range(3)]
            for copy in rs:
                start(None, copy)
        else:
            rs = []
            o_ck[:, i * HD:(i + 1) * HD] = tail[:, :HD]
            o_cv[:, i * HD:(i + 1) * HD] = tail[:, HD:]
        acc[i] = shared[:2 * T]
        o_att[0, 0, :, mine(i)] = ats[i, 0, rows(s * T), :]
        o_dq[0, 0, :, mine(i)] = ats[i, 1, rows(s * T), :]
        returns[i] = (to_below, to_above, to_side, rs)

    def finish(i):
        to_below, to_above, to_side, rs = returns[i]
        arrived(up_ok, [to_below])
        arrived(down_ok, [to_above])
        for j in range(plan.sides):
            arrived(side_ok[j], [to_side[plan.opposite(j)]])
        for t in range(2):
            total = acc[i, pl.ds(t * T, T), :] + cr[i, pl.ds((1 - t) * T, T), :].astype(F32)
            for j in range(plan.sides):
                total = total + cr[i, pl.ds(2 * T + 2 * T * j + t * T, T), :].astype(F32)
            fs[i, pl.ds(t * T, T), :] = total.astype(BF16)
        made = [remote("dk", i, fs.at[i, rows((1 - s) * T), pl.ds(0, HD)], o_dk.at[0, 0, :, mine(i)], partner),
                remote("dv", i, fs.at[i, rows((1 - s) * T), pl.ds(HD, HD)], o_dv.at[0, 0, :, mine(i)], partner)]
        for copy in made:
            start(None, copy)
            last_recv.append(copy)
        o_dk[0, 0, :, mine(i)] = fs[i, rows(s * T), :HD]
        o_dv[0, 0, :, mine(i)] = fs[i, rows(s * T), HD:]

    cap_parts = {}

    def caption(i):
        if not plan.inside:
            return
        for copy in returns[i][3]:
            copy.wait_recv()
        at = rows((2 * k + band) * plan.part, plan.part)
        total = caps[i, at, :]
        for n in range(3):
            total = total + crv[i, n].astype(F32)
        fp[i] = total.astype(BF16)
        k_src, v_src = fp.at[i, :, pl.ds(0, HD)], fp.at[i, :, pl.ds(HD, HD)]
        ahead = []
        for n, dev in enumerate([partner] + mates):
            pair = [remote("fk%d" % n, i, k_src, o_ck.at[at, mine(i)], dev),
                    remote("fv%d" % n, i, v_src, o_cv.at[at, mine(i)], dev)]
            for copy in pair:
                start(None, copy)
            if n == 0:
                cap_parts[i] = pair
            else:
                last_recv.extend(pair)
        o_ck[at, mine(i)] = fp[i, :, :HD]
        o_cv[at, mine(i)] = fp[i, :, HD:]

    def pass_on(i):
        if not plan.inside:
            return
        for copy in cap_parts[i]:
            copy.wait_recv()
        at = rows((2 * k + band) * plan.part, plan.part)
        for n, dev in enumerate(mates):
            pair = [remote("pk%d" % n, i, o_ck.at[at, his(i)], o_ck.at[at, his(i)], dev),
                    remote("pv%d" % n, i, o_cv.at[at, his(i)], o_cv.at[at, his(i)], dev)]
            for copy in pair:
                start(None, copy)
                last_recv.append(copy)

    for i in range(G):
        attend(i)
        if i >= 1:
            finish(i - 1)
            caption(i - 1)
        if i >= 2:
            pass_on(i - 2)
    finish(G - 1)
    caption(G - 1)
    for i in range(max(G - 2, 0), G):
        pass_on(i)
    for copy in last_recv:
        copy.wait_recv()
    for ok, copy in sends:
        when(ok, copy.wait_send)


def kinds_of(plan):
    names = ["link", "k", "v", "q", "g", "att", "dq", "dk", "dv", "rb", "ra"]
    names += [d + n for d in ("up", "down") for n in "kv"]
    for j in range(plan.sides):
        names += ["%s%d%s" % (d, j, n) for d in ("first", "second") for n in "kv"] + ["rs%d" % j]
    if plan.inside:
        names += ["cr%d" % n for n in range(3)]
        names += ["%s%d" % (d, n) for d in ("fk", "fv") for n in range(4)]
        names += ["%s%d" % (d, n) for d in ("pk", "pv") for n in range(3)]
    return names


def body(mesh_shape, queries, keys, values, grad_out, caption_keys, caption_values, caption_mask, kept):
    T, C = queries.shape[2], caption_keys.shape[0]
    width = queries.shape[3]
    plan = Plan(mesh_shape, T, C, width // HD)
    for name in kinds_of(plan):
        plan.number(name, 0)
    G = plan.group
    count = len(plan.kinds) * G
    tile_out = jax.ShapeDtypeStruct(queries.shape, BF16)
    cap_out = (jax.ShapeDtypeStruct((C, width), BF16) if plan.inside
               else jax.ShapeDtypeStruct((C, G * HD), F32))
    hbm = pl.BlockSpec(memory_space=pltpu.HBM)
    vmem = pl.BlockSpec(memory_space=pltpu.VMEM)
    smem = pl.BlockSpec(memory_space=pltpu.SMEM)
    cap_rows = C if plan.inside else 16
    part = plan.part if plan.inside else 16
    side_rows = 2 * T + 2 * T * plan.sides
    outs = pl.pallas_call(
        functools.partial(kernel, plan, 1.0 / math.sqrt(HD)),
        out_shape=(tile_out,) * 4 + (cap_out,) * 2,
        in_specs=[hbm] * 6 + [vmem, smem],
        out_specs=(vmem,) * 6,
        scratch_shapes=[
            pltpu.VMEM((G, plan.rows, HD), BF16),
            pltpu.VMEM((G, plan.rows, HD), BF16),
            pltpu.VMEM((G, 2 * T, HD), BF16),
            pltpu.VMEM((G, 2 * T, HD), BF16),
            pltpu.VMEM((2, 8, 128), F32),
            pltpu.VMEM((G, 2 * T, 2 * HD), F32),
            pltpu.VMEM((G, cap_rows, 2 * HD), F32),
            pltpu.VMEM((G, side_rows, 2 * HD), BF16),
            pltpu.VMEM((G, side_rows, 2 * HD), BF16),
            pltpu.VMEM((G, cap_rows, 2 * HD), BF16),
            pltpu.VMEM((G, 3, part, 2 * HD), BF16),
            pltpu.VMEM((G, part, 2 * HD), BF16),
            pltpu.VMEM((G, 2 * T, 2 * HD), BF16),
            pltpu.VMEM((G, 2, 2 * T, HD), BF16),
            pltpu.SemaphoreType.DMA((6 * G,)),
            pltpu.SemaphoreType.DMA((count,)),
            pltpu.SemaphoreType.DMA((count,)),
        ],
        compiler_params=pltpu.CompilerParams(
            collective_id=0, has_side_effects=True, vmem_limit_bytes=40 * 1024 * 1024),
    )(queries, keys, values, grad_out, caption_keys, caption_values,
      caption_mask.reshape(1, C), kept)
    if plan.inside:
        return outs
    at = lax.rem(lax.axis_index("tm"), 2) * (G * HD)
    summed = [lax.dynamic_update_slice(jnp.zeros((C, width), F32), part, (0, at)) for part in outs[4:]]
    summed = lax.psum(tuple(summed), ("tm", "height"))
    return outs[:4] + tuple(x.astype(BF16) for x in summed)


def solution(mesh):
    tiles = P("tm", "height", None, "head")
    caption = P(None, "head")
    return jax.shard_map(
        functools.partial(body, dict(mesh.shape)),
        mesh=mesh,
        in_specs=(tiles,) * 4 + (caption,) * 2 + (P(), P("tm", "height", None)),
        out_specs=(tiles,) * 4 + (caption,) * 2,
        check_vma=False,
    )
```

time: 164 us -> 46.6 us (0.28); the launches traced: 161 us -> 46.3 us
  blocking collectives: 58.3 us -> 0 us
  Pallas kernels: 0 us -> 35 us
  local copies, waits for them, and re-layouts: 45.1 us -> 10.6 us
  starting transfers between devices: 19.1 us -> 0 us
  waiting for transfers between devices: 15.5 us -> 0 us
  other arithmetic: 11.6 us -> 0 us
  matrix products: 10.5 us -> 0 us
    psum x1 -> x0, blocking collectives: 58.3 us -> none  [body(): lax.psum((caption_dk, caption_dv), ('tm', 'height'))]
    pallas_call x0 -> x1, Pallas kernels: none -> 35 us  [body(): pl.pallas_call(functools.partial(kernel, plan, 1.0 / math.sqrt(HD)), out_...]
    ppermute x8 -> x0, starting transfers between devices: 19.1 us -> none  [the longest x4 9.19 us: from_behind(): return lax.ppermute(shard, axis, pairs)]
    ppermute x8 -> x0, waiting for transfers between devices: 15.5 us -> none  [the longest x2 11 us: padded(): lax.ppermute(lax.slice_in_dim(block, 0, width, axis=dim), axis, backward)]
    dot_general x18 -> x0, matrix products: 10.5 us -> none  [the longest x3 3.65 us: body(): jnp.einsum('grk,rgd->kgd', picked_scores, query_heads, preferred_element_...]
    unnamed x67 -> x22, local copies, waits for them, and re-layouts: 18.4 us -> 10.6 us
    mul x3 -> x0, local copies, waits for them, and re-layouts: 7.3 us -> none  [body(): jnp.einsum('grk,rgd->kgd', picked_scores, query_heads, preferred_element_...]
    slice x13 -> x0, local copies, waits for them, and re-layouts: 7.17 us -> none  [the longest x10 4.2 us: head_slice(): lax.slice_in_dim(array, start_head * HD, (start_head + head_group) * HD,...]
  transfers between devices with their start and end apart: 8 -> 0, of which waited for: 3 -> 0; matrix products, arithmetic and copies ran while one was open for 13% -> 0% of each run, Pallas kernels for 0% -> 0%
where the time goes in v1:
time: 46.6 us; the launch traced here: 46.3 us
  Pallas kernels  35 us (75%)
  local copies, waits for them, and re-layouts  10.6 us (23%)
  between operations  0.67 us (1%)
    pallas_call x1, Pallas kernels, body(): pl.pallas_call(functools.partial(kernel, plan, 1.0 / math.sqrt(HD)), out_...  35 us
    unnamed x22, local copies, waits for them, and re-layouts  10.6 us

profile of v1, /device:TPU:0, one launch (start us, length us, event | category | flops | bytes accessed | tf_op | source)
XLA Modules:
  0.0 46.3 jit_solution(13691898512026485252)
XLA Ops:
  0.6 0.0 copy-start.7
  0.6 0.0 copy-start.6
  0.7 0.6 %copy-done.7 = s32[1,1,4]{2,1,0:T(1,128)S(1)} copy-done((s32[1,1,4]{2,1,0:T(1,128)S(1)}, s32[1,1,4]{2,1,0:T(1,128)}, u32[]{:S(2)}) %copy-start.7) | copy-done | bytes 40
  1.3 0.0 copy-done.6
  1.3 0.0 copy-start
  1.3 1.0 %copy-done = bf16[256,768]{1,0:T(8,128)(2,1)S(1)} copy-done((bf16[256,768]{1,0:T(8,128)(2,1)S(1)}, bf16[256,768]{1,0:T(8,128)(2,1)}, u32[]{:S(2)}) %copy-start) | copy-done | bytes 393240
  2.3 0.0 copy-start.1
  2.3 1.0 %copy-done.1 = bf16[256,768]{1,0:T(8,128)(2,1)S(1)} copy-done((bf16[256,768]{1,0:T(8,128)(2,1)S(1)}, bf16[256,768]{1,0:T(8,128)(2,1)}, u32[]{:S(2)}) %copy-start.1) | copy-done | bytes 393240
  3.3 0.0 copy-start.2
  3.3 0.9 %copy-done.2 = bf16[1,1,128,768]{3,2,1,0:T(8,128)(2,1)S(1)} copy-done((bf16[1,1,128,768]{3,2,1,0:T(8,128)(2,1)S(1)}, bf16[1,1,128,768]{3,2,1,0:T(8,128)(2,1)}, u32[]{:S(2)}) %copy-start.2) | copy-done | bytes 196632
  4.3 0.0 copy-start.3
  4.3 0.9 %copy-done.3 = bf16[1,1,128,768]{3,2,1,0:T(8,128)(2,1)S(1)} copy-done((bf16[1,1,128,768]{3,2,1,0:T(8,128)(2,1)S(1)}, bf16[1,1,128,768]{3,2,1,0:T(8,128)(2,1)}, u32[]{:S(2)}) %copy-start.3) | copy-done | bytes 196632
  5.2 0.0 copy-start.4
  5.2 0.9 %copy-done.4 = bf16[1,1,128,768]{3,2,1,0:T(8,128)(2,1)S(1)} copy-done((bf16[1,1,128,768]{3,2,1,0:T(8,128)(2,1)S(1)}, bf16[1,1,128,768]{3,2,1,0:T(8,128)(2,1)}, u32[]{:S(2)}) %copy-start.4) | copy-done | bytes 196632
  6.1 0.0 copy-start.5
  6.1 0.9 %copy-done.5 = bf16[1,1,128,768]{3,2,1,0:T(8,128)(2,1)S(1)} copy-done((bf16[1,1,128,768]{3,2,1,0:T(8,128)(2,1)S(1)}, bf16[1,1,128,768]{3,2,1,0:T(8,128)(2,1)}, u32[]{:S(2)}) %copy-start.5) | copy-done | bytes 196632
  7.0 35.0 %shard_map.127 = (bf16[1,1,128,768]{3,2,1,0:T(8,128)(2,1)S(1)}, bf16[1,1,128,768]{3,2,1,0:T(8,128)(2,1)S(1)}, bf16[1,1,128,768]{3,2,1,0:T(8,128)(2,1)S(1)}, bf16...) custom-call(bf16[1,1,128,768]{3,2,1,0:T(8,128)(2,1)S(1)} %copy-done.2, ...), custom_call_target="tpu_custom_call" | custom-call | tf_op jit(solution)/shard_map/pallas_call | solution.py:413
  42.1 0.7 %copy.20 = bf16[1,1,128,768]{3,2,1,0:T(8,128)(2,1)} copy(bf16[1,1,128,768]{3,2,1,0:T(8,128)(2,1)S(1)} %get-tuple-element.12) | data formatting | bytes 393216
  42.8 0.7 %copy.21 = bf16[1,1,128,768]{3,2,1,0:T(8,128)(2,1)} copy(bf16[1,1,128,768]{3,2,1,0:T(8,128)(2,1)S(1)} %get-tuple-element.13) | data formatting | bytes 393216
  43.4 0.7 %copy.22 = bf16[1,1,128,768]{3,2,1,0:T(8,128)(2,1)} copy(bf16[1,1,128,768]{3,2,1,0:T(8,128)(2,1)S(1)} %get-tuple-element.14) | data formatting | bytes 393216
  44.1 0.7 %copy.23 = bf16[1,1,128,768]{3,2,1,0:T(8,128)(2,1)} copy(bf16[1,1,128,768]{3,2,1,0:T(8,128)(2,1)S(1)} %get-tuple-element.15) | data formatting | bytes 393216
  44.8 0.7 %copy.24 = bf16[256,768]{1,0:T(8,128)(2,1)} copy(bf16[256,768]{1,0:T(8,128)(2,1)S(1)} %get-tuple-element.16) | data formatting | bytes 786432
  45.5 0.7 %copy.25 = bf16[256,768]{1,0:T(8,128)(2,1)} copy(bf16[256,768]{1,0:T(8,128)(2,1)S(1)} %get-tuple-element.17) | data formatting | bytes 786432
Async XLA Ops:
  0.6 0.7 %copy-start.7 = (s32[1,1,4]{2,1,0:T(1,128)S(1)}, s32[1,1,4]{2,1,0:T(1,128)}, u32[]{:S(2)}) copy-start(s32[1,1,4]{2,1,0:T(1,128)} %kept_ref.1) | copy-start | bytes 52
  0.6 0.7 %copy-start.6 = (s32[256]{0:T(256)S(1)}, s32[256]{0:T(256)}, u32[]{:S(2)}) copy-start(s32[256]{0:T(256)} %param.14) | copy-start | bytes 3076
  1.3 1.0 %copy-start = (bf16[256,768]{1,0:T(8,128)(2,1)S(1)}, bf16[256,768]{1,0:T(8,128)(2,1)}, u32[]{:S(2)}) copy-start(bf16[256,768]{1,0:T(8,128)(2,1)} %ck_in.1) | copy-start | bytes 1179652
  2.3 1.0 %copy-start.1 = (bf16[256,768]{1,0:T(8,128)(2,1)S(1)}, bf16[256,768]{1,0:T(8,128)(2,1)}, u32[]{:S(2)}) copy-start(bf16[256,768]{1,0:T(8,128)(2,1)} %cv_in.1) | copy-start | bytes 1179652
  3.3 0.9 %copy-start.2 = (bf16[1,1,128,768]{3,2,1,0:T(8,128)(2,1)S(1)}, bf16[1,1,128,768]{3,2,1,0:T(8,128)(2,1)}, u32[]{:S(2)}) copy-start(bf16[1,1,128,768]{3,2,1,0:T(8,128)(2,1)} %q_in.1) | copy-start | bytes 589828
  4.3 0.9 %copy-start.3 = (bf16[1,1,128,768]{3,2,1,0:T(8,128)(2,1)S(1)}, bf16[1,1,128,768]{3,2,1,0:T(8,128)(2,1)}, u32[]{:S(2)}) copy-start(bf16[1,1,128,768]{3,2,1,0:T(8,128)(2,1)} %k_in.1) | copy-start | bytes 589828
  5.2 0.9 %copy-start.4 = (bf16[1,1,128,768]{3,2,1,0:T(8,128)(2,1)S(1)}, bf16[1,1,128,768]{3,2,1,0:T(8,128)(2,1)}, u32[]{:S(2)}) copy-start(bf16[1,1,128,768]{3,2,1,0:T(8,128)(2,1)} %v_in.1) | copy-start | bytes 589828
  6.1 0.9 %copy-start.5 = (bf16[1,1,128,768]{3,2,1,0:T(8,128)(2,1)S(1)}, bf16[1,1,128,768]{3,2,1,0:T(8,128)(2,1)}, u32[]{:S(2)}) copy-start(bf16[1,1,128,768]{3,2,1,0:T(8,128)(2,1)} %g_in.1) | copy-start | bytes 589828

commit v2 on v1

--- a/solution.py
+++ b/solution.py
@@ -12,6 +12,7 @@
 NEG = -1e30
 F32 = jnp.float32
 BF16 = jnp.bfloat16
+ORDER = ["att", "dq", "dk", "dv", "ck", "cv"]
 MESH = pl.DeviceIdType.MESH
 
 
@@ -42,10 +43,12 @@
         return base * self.group + i
 
 
-def kernel(plan, scale, q_in, k_in, v_in, g_in, ck_in, cv_in, mask_ref, kept_ref,
-           o_att, o_dq, o_dk, o_dv, o_ck, o_cv,
-           kb, vb, qb, gb, links, acc, caps, cs, cr, cp, crv, fp, fs, ats,
-           local_sem, send_sem, recv_sem):
+def kernel(plan, scale, *refs):
+    hbm_in, (mask_ref, kept_ref), hbm_out = refs[:6], refs[6:8], refs[8:14]
+    q_in, k_in, v_in, g_in, ck_in, cv_in = here_in = refs[14:20]
+    o_att, o_dq, o_dk, o_dv, o_ck, o_cv = here_out = refs[20:26]
+    (kb, vb, qb, gb, links, acc, caps, cs, cr, cp, crv, fp, fs, ats,
+     stage_sem, local_sem, send_sem, recv_sem) = refs[26:]
     T, G, C = plan.tile, plan.group, plan.cap
     tm, band, head = lax.axis_index("tm"), lax.axis_index("height"), lax.axis_index("head")
     s, k = lax.rem(tm, 2), lax.div(tm, 2)
@@ -94,6 +97,10 @@
         when(ok, copy.start)
         sends.append((ok, copy))
 
+    staged = [pltpu.make_async_copy(hbm_in[n], here_in[n], stage_sem.at[n]) for n in range(6)]
+    for n in (1, 2, 0, 3, 4, 5):
+        staged[n].start()
+
     own_kv, own_qg = [], []
     for i in range(G):
         group = [
@@ -105,8 +112,6 @@
             (cv_in.at[:, mine(i)], vb.at[i, pl.ds(plan.caps, C)]),
         ]
         made = [pltpu.make_async_copy(a, b, local_sem.at[6 * i + n]) for n, (a, b) in enumerate(group)]
-        for copy in made:
-            copy.start()
         own_kv.append(made[:2])
         own_qg.append(made[2:])
 
@@ -151,6 +156,8 @@
     link_copy = remote("link", 0, links.at[s], links.at[s], partner)
     start(None, link_copy)
     swap_kv, swap_qg = [], []
+    staged[1].wait()
+    staged[2].wait()
     for i in range(G):
         made = [remote("k", i, k_in.at[0, 0, :, his(i)], kb.at[i, own_slot], partner),
                 remote("v", i, v_in.at[0, 0, :, his(i)], vb.at[i, own_slot], partner)]
@@ -158,11 +165,21 @@
             start(None, copy)
         swap_kv.append(made)
     for i in range(G):
+        for copy in own_kv[i]:
+            copy.start()
+    staged[0].wait()
+    staged[3].wait()
+    for i in range(G):
         made = [remote("q", i, q_in.at[0, 0, :, his(i)], qb.at[i, rows(s * T)], partner),
                 remote("g", i, g_in.at[0, 0, :, his(i)], gb.at[i, rows(s * T)], partner)]
         for copy in made:
             start(None, copy)
         swap_qg.append(made)
+    staged[4].wait()
+    staged[5].wait()
+    for i in range(G):
+        for copy in own_qg[i]:
+            copy.start()
 
     up, down = [], []
     side_first = [[] for _ in range(plan.sides)]
@@ -231,8 +248,14 @@
     def dot(a, b, dims):
         return lax.dot_general(a, b, (dims, ((), ())), preferred_element_type=F32)
 
-    last_recv = []
+    last_recv = {name: [] for name in ORDER}
     returns = {}
+    kept_here = {name: [] for name in ORDER}
+
+    def keep(n, i, src, dst):
+        copy = pltpu.make_async_copy(src, dst, local_sem.at[6 * i + n])
+        copy.start()
+        kept_here[ORDER[n]].append(copy.wait)
 
     def attend(i):
         for copy in own_qg[i]:
@@ -264,9 +287,9 @@
             grads.append(jnp.concatenate([dk, dv], axis=1))
         made = [remote("att", i, ats.at[i, 0, rows((1 - s) * T)], o_att.at[0, 0, :, mine(i)], partner),
                 remote("dq", i, ats.at[i, 1, rows((1 - s) * T)], o_dq.at[0, 0, :, mine(i)], partner)]
-        for copy in made:
+        for name, copy in zip(("att", "dq"), made):
             start(None, copy)
-            last_recv.append(copy)
+            last_recv[name].append(copy.wait_recv)
         low, high = grads
         mid = plan.lo
         cs[i, pl.ds(0, T), :] = low[:T].astype(BF16)
@@ -302,8 +325,8 @@
             o_ck[:, i * HD:(i + 1) * HD] = tail[:, :HD]
             o_cv[:, i * HD:(i + 1) * HD] = tail[:, HD:]
         acc[i] = shared[:2 * T]
-        o_att[0, 0, :, mine(i)] = ats[i, 0, rows(s * T), :]
-        o_dq[0, 0, :, mine(i)] = ats[i, 1, rows(s * T), :]
+        keep(0, i, ats.at[i, 0, rows(s * T)], o_att.at[0, 0, :, mine(i)])
+        keep(1, i, ats.at[i, 1, rows(s * T)], o_dq.at[0, 0, :, mine(i)])
         returns[i] = (to_below, to_above, to_side, rs)
 
     def finish(i):
@@ -319,11 +342,11 @@
             fs[i, pl.ds(t * T, T), :] = total.astype(BF16)
         made = [remote("dk", i, fs.at[i, rows((1 - s) * T), pl.ds(0, HD)], o_dk.at[0, 0, :, mine(i)], partner),
                 remote("dv", i, fs.at[i, rows((1 - s) * T), pl.ds(HD, HD)], o_dv.at[0, 0, :, mine(i)], partner)]
-        for copy in made:
+        for name, copy in zip(("dk", "dv"), made):
             start(None, copy)
-            last_recv.append(copy)
-        o_dk[0, 0, :, mine(i)] = fs[i, rows(s * T), :HD]
-        o_dv[0, 0, :, mine(i)] = fs[i, rows(s * T), HD:]
+            last_recv[name].append(copy.wait_recv)
+        keep(2, i, fs.at[i, rows(s * T), pl.ds(0, HD)], o_dk.at[0, 0, :, mine(i)])
+        keep(3, i, fs.at[i, rows(s * T), pl.ds(HD, HD)], o_dv.at[0, 0, :, mine(i)])
 
     cap_parts = {}
 
@@ -347,9 +370,10 @@
             if n == 0:
                 cap_parts[i] = pair
             else:
-                last_recv.extend(pair)
-        o_ck[at, mine(i)] = fp[i, :, :HD]
-        o_cv[at, mine(i)] = fp[i, :, HD:]
+                for name, copy in zip(("ck", "cv"), pair):
+                    last_recv[name].append(copy.wait_recv)
+        keep(4, i, k_src, o_ck.at[at, mine(i)])
+        keep(5, i, v_src, o_cv.at[at, mine(i)])
 
     def pass_on(i):
         if not plan.inside:
@@ -360,9 +384,9 @@
         for n, dev in enumerate(mates):
             pair = [remote("pk%d" % n, i, o_ck.at[at, his(i)], o_ck.at[at, his(i)], dev),
                     remote("pv%d" % n, i, o_cv.at[at, his(i)], o_cv.at[at, his(i)], dev)]
-            for copy in pair:
+            for name, copy in zip(("ck", "cv"), pair):
                 start(None, copy)
-                last_recv.append(copy)
+                last_recv[name].append(copy.wait_recv)
 
     for i in range(G):
         attend(i)
@@ -375,8 +399,17 @@
     caption(G - 1)
     for i in range(max(G - 2, 0), G):
         pass_on(i)
-    for copy in last_recv:
-        copy.wait_recv()
+    written = []
+    for names in (("att", "dq"), ("dk", "dv"), ("ck", "cv")):
+        for name in names:
+            for copy in last_recv[name] + kept_here[name]:
+                copy()
+            n = ORDER.index(name)
+            made = pltpu.make_async_copy(here_out[n], hbm_out[n], stage_sem.at[n])
+            made.start()
+            written.append(made)
+    for copy in written:
+        copy.wait()
     for ok, copy in sends:
         when(ok, copy.wait_send)
 
@@ -414,8 +447,10 @@
         functools.partial(kernel, plan, 1.0 / math.sqrt(HD)),
         out_shape=(tile_out,) * 4 + (cap_out,) * 2,
         in_specs=[hbm] * 6 + [vmem, smem],
-        out_specs=(vmem,) * 6,
-        scratch_shapes=[
+        out_specs=(hbm,) * 6,
+        scratch_shapes=[pltpu.VMEM(a.shape, BF16) for a in (
+            queries, keys, values, grad_out, caption_keys, caption_values)] + [
+            pltpu.VMEM(a.shape, a.dtype) for a in (tile_out,) * 4 + (cap_out,) * 2] + [
             pltpu.VMEM((G, plan.rows, HD), BF16),
             pltpu.VMEM((G, plan.rows, HD), BF16),
             pltpu.VMEM((G, 2 * T, HD), BF16),
@@ -430,20 +465,47 @@
             pltpu.VMEM((G, part, 2 * HD), BF16),
             pltpu.VMEM((G, 2 * T, 2 * HD), BF16),
             pltpu.VMEM((G, 2, 2 * T, HD), BF16),
+            pltpu.SemaphoreType.DMA((6,)),
             pltpu.SemaphoreType.DMA((6 * G,)),
             pltpu.SemaphoreType.DMA((count,)),
             pltpu.SemaphoreType.DMA((count,)),
         ],
         compiler_params=pltpu.CompilerParams(
-            collective_id=0, has_side_effects=True, vmem_limit_bytes=40 * 1024 * 1024),
+            collective_id=0, has_side_effects=True, vmem_limit_bytes=58 * 1024 * 1024),
     )(queries, keys, values, grad_out, caption_keys, caption_values,
       caption_mask.reshape(1, C), kept)
     if plan.inside:
-        return outs
+        return place(outs)
     at = lax.rem(lax.axis_index("tm"), 2) * (G * HD)
     summed = [lax.dynamic_update_slice(jnp.zeros((C, width), F32), part, (0, at)) for part in outs[4:]]
     summed = lax.psum(tuple(summed), ("tm", "height"))
-    return outs[:4] + tuple(x.astype(BF16) for x in summed)
+    return place(outs[:4]) + tuple(x.astype(BF16) for x in summed)
+
+
+def place_kernel(*refs):
+    count = (len(refs) - 1) // 3
+    sources, targets, between, sem = refs[:count], refs[count:2 * count], refs[2 * count:3 * count], refs[-1]
+    first = [pltpu.make_async_copy(sources[n], between[n], sem.at[0, n]) for n in range(count)]
+    second = [pltpu.make_async_copy(between[n], targets[n], sem.at[1, n]) for n in range(count)]
+    for copy in first:
+        copy.start()
+    for n in range(count):
+        first[n].wait()
+        second[n].start()
+    for copy in second:
+        copy.wait()
+
+
+def place(arrays):
+    return tuple(pl.pallas_call(
+        place_kernel,
+        out_shape=tuple(jax.ShapeDtypeStruct(a.shape, a.dtype) for a in arrays),
+        in_specs=[pl.BlockSpec(memory_space=pltpu.HBM)] * len(arrays),
+        out_specs=(pl.BlockSpec(memory_space=pltpu.HBM),) * len(arrays),
+        scratch_shapes=[pltpu.VMEM(a.shape, a.dtype) for a in arrays]
+        + [pltpu.SemaphoreType.DMA((2, len(arrays)))],
+        compiler_params=pltpu.CompilerParams(vmem_limit_bytes=58 * 1024 * 1024),
+    )(*arrays))
 
 
 def solution(mesh):

time: 46.6 us -> 39.2 us (0.84)
  local copies, waits for them, and re-layouts: 10.6 us -> 0 us
  Pallas kernels: 35 us -> 38.4 us
    unnamed x22 -> x0, local copies, waits for them, and re-layouts: 10.6 us -> none
    pallas_call x0 -> x1, Pallas kernels: none -> 2.33 us  [place(): pl.pallas_call(place_kernel, out_shape=tuple((jax.ShapeDtypeStruct(a.shap...]
    pallas_call x1, Pallas kernels: 35 us -> 36.1 us  [body(): pl.pallas_call(functools.partial(kernel, plan, 1.0 / math.sqrt(HD)), out_...]
where the time goes in v2:
time: 39.2 us; the launch traced here: 39 us
  Pallas kernels  38.4 us (98%)
  between operations  0.64 us (2%)
    pallas_call x1, Pallas kernels, body(): pl.pallas_call(functools.partial(kernel, plan, 1.0 / math.sqrt(HD)), out_...  36.1 us
    pallas_call x1, Pallas kernels, place(): pl.pallas_call(place_kernel, out_shape=tuple((jax.ShapeDtypeStruct(a.shap...  2.33 us

profile of v2, /device:TPU:0, one launch (start us, length us, event | category | flops | bytes accessed | tf_op | source)
XLA Modules:
  0.0 39.0 jit_solution(772876510370274685)
XLA Ops:
  0.6 36.1 %shard_map.127 = (bf16[1,1,128,768]{3,2,1,0:T(8,128)(2,1)}, bf16[1,1,128,768]{3,2,1,0:T(8,128)(2,1)}, bf16[1,1,128,768]{3,2,1,0:T(8,128)(2,1)}, bf16[1,1,128,768...) custom-call(bf16[1,1,128,768]{3,2,1,0:T(8,128)(2,1)} %refs_0_.1, ...), custom_call_target="tpu_custom_call" | custom-call | tf_op jit(solution)/shard_map/pallas_call | solution.py:446
  36.7 2.3 %shard_map.128 = (bf16[1,1,128,768]{3,2,1,0:T(8,128)(2,1)}, bf16[1,1,128,768]{3,2,1,0:T(8,128)(2,1)}, bf16[1,1,128,768]{3,2,1,0:T(8,128)(2,1)}, bf16[1,1,128,768...) custom-call(bf16[1,1,128,768]{3,2,1,0:T(8,128)(2,1)} %get-tuple-element.12.refs_0_, ...), custom_call_target="tpu_custom_call" | custom-call | tf_op jit(solution)/shard_map/pallas_call | solution.py:500
